TPU v7x, 256 devices: a whole 4x4x8 slice. The times are simulated.
256 devices in a mesh: enc: 16 (over x, y), blk: 16 (over z, core).
Axes of the slice: x: 4, y: 4, z: 8, core: 2. Of those that a mesh axis runs over, the one named last changes fastest.
Arguments:
- observations: bfloat16 [131072, 128], P(('enc', 'blk')), may hold values from -6 to 6
- lon_index: int32 [256, 512], P(('enc', 'blk')), may hold values from 0 to 1439
- live_count: int32 [256, 256], P(('enc', 'blk')), may hold values from 0 to 2, as said below
- w_in: bfloat16 [128, 512], replicated, may hold values from -0.5 to 0.5
- w_out: bfloat16 [512, 512], replicated, may hold values from -0.25 to 0.25
- w_spec: float32 [256, 512], replicated, may hold values from -4 to 4
- north: float32 [256, 512], P(('enc', 'blk')), may hold values from -0.8 to 0.8
- south: float32 [256, 512], P(('enc', 'blk')), may hold values from -0.8 to 0.8
- w_mix: bfloat16 [512, 512], replicated, may hold values from -0.25 to 0.25
- loss_sensitivity: bfloat16 [256, 1440, 512], P(('enc', 'blk')), may hold values from -6 to 6
Outputs:
- predicted_state: bfloat16 [256, 1440, 512], P(('enc', 'blk'))
- entry_matrix_slope: float32 [128, 512], replicated
- exit_matrix_slope: float32 [512, 512], replicated
- blend_matrix_slope: float32 [512, 512], replicated
- observation_slope: bfloat16 [131072, 128], P(('enc', 'blk'))
Inputs may be any that keep to these rules, and one draw needn't show every extreme that they name: In every draw some cycle r has live_count[r, s] = 2 for every source s.
All inputs are finite; a program needn't handle non-finite values.
Results may differ from a plain program's by a relative error of at most 0.0095.
Values may be sent and summed in bfloat16 or wider, within the bound.
No kernel may reach another device: no remote copies, remote signals or barrier semaphores. Data moves between devices by JAX's collectives and lax.ppermute only.
A program may use at most 64 MiB of HBM per device.

v0:
```python
import math
import jax
import jax.numpy as jnp
from jax import lax
from jax.sharding import PartitionSpec as P

CODE_BREADTH = 512
LON = 1440
MODES = 128
CAP = 2


def extended(block, sides, width):
    for axis, dim in sides:
        count = lax.axis_size(axis)
        forward = [(i, i + 1) for i in range(count - 1)]
        backward = [(target, source) for source, target in forward]
        low = lax.ppermute(
            lax.slice_in_dim(block, block.shape[dim] - width, None, axis=dim), axis, forward
        )
        high = lax.ppermute(lax.slice_in_dim(block, 0, width, axis=dim), axis, backward)
        block = jnp.concatenate([low, block, high], axis=dim)
    return block


def from_behind(value, axis, steps):
    count = lax.axis_size(axis)
    initial, last = (max(0, -steps), min(count, count - steps))
    return lax.ppermute(value, axis, [(source, source + steps) for source in range(initial, last)])


def tables():
    wavenum = jnp.arange(MODES, dtype=jnp.int32)
    lon_pos = jnp.arange(LON, dtype=jnp.int32)
    phases = (wavenum[:, None] * lon_pos[None, :] % LON).astype(jnp.float32) * (2.0 * math.pi / LON)
    forward = jnp.concatenate([jnp.cos(phases), -jnp.sin(phases)], 0).astype(jnp.bfloat16)
    weight = jnp.where(wavenum == 0, 1.0, 2.0).astype(jnp.float32) / LON
    inverse = jnp.concatenate(
        [jnp.cos(phases) * weight[:, None], -jnp.sin(phases) * weight[:, None]], 0
    ).T.astype(jnp.bfloat16)
    return (forward, inverse)


def silu_grad(values):
    logistic = jax.nn.sigmoid(values)
    return logistic * (1.0 + values * (1.0 - logistic))


def cell_table(lon_row, count_row):
    is_live = (jnp.arange(CAP, dtype=jnp.int32)[None, :] < count_row[:, None]).reshape(-1)
    matches = (lon_row[None, :] == jnp.arange(LON, dtype=jnp.int32)[:, None]) & is_live[None, :]
    return (matches.astype(jnp.bfloat16), jnp.sum(matches.astype(jnp.float32), axis=1))


def encode(rows, w_in, w_out):
    pre1 = jnp.dot(rows, w_in, preferred_element_type=jnp.float32)
    hidden = jax.nn.silu(pre1).astype(jnp.bfloat16)
    latent = jnp.dot(hidden, w_out, preferred_element_type=jnp.float32).astype(jnp.bfloat16)
    return (pre1, hidden, latent)


def encoder_grads(rows, pre1, hidden, grad_latent, w_in, w_out):
    out_local = jnp.dot(hidden.T, grad_latent, preferred_element_type=jnp.float32)
    grad_hidden = jnp.dot(grad_latent, w_out.T, preferred_element_type=jnp.float32)
    grad_pre1 = (grad_hidden * silu_grad(pre1)).astype(jnp.bfloat16)
    in_local = jnp.dot(rows.T, grad_pre1, preferred_element_type=jnp.float32)
    row_grads = jnp.dot(grad_pre1, w_in.T, preferred_element_type=jnp.float32).astype(jnp.bfloat16)
    return (in_local, out_local, row_grads)


def shards(
    observations, lon_index, live_count, w_in, w_out, w_spec, north, south, w_mix, loss_sensitivity
):
    enc_count = lax.axis_size("enc")
    blk_count = lax.axis_size("blk")
    devices = enc_count * blk_count
    slot_total = observations.shape[0]
    forward, inverse = tables()
    pre1, hidden, latent = encode(observations, w_in, w_out)
    outgoing = latent.reshape(enc_count, blk_count, CAP, CODE_BREADTH)
    arrived = lax.all_to_all(
        lax.all_to_all(outgoing, "enc", split_axis=0, concat_axis=0, tiled=True),
        "blk",
        split_axis=1,
        concat_axis=1,
        tiled=True,
    )
    lat_rows = arrived.reshape(slot_total, CODE_BREADTH)
    onehot, occupancy = cell_table(lon_index[0], live_count[0])
    denom = jnp.maximum(occupancy, 1.0)[:, None]
    grid_sum = jnp.dot(onehot, lat_rows, preferred_element_type=jnp.float32)
    resampled_field = (grid_sum / denom).astype(jnp.bfloat16)
    spectrum = jnp.dot(forward, resampled_field, preferred_element_type=jnp.float32)
    border = extended(resampled_field[None], ((("enc", "blk"), 0),), 1)
    spec_prev = jnp.dot(forward, border[0], preferred_element_type=jnp.float32)
    spec_next = jnp.dot(forward, border[2], preferred_element_type=jnp.float32)
    north_row = north[0][None, :]
    south_row = south[0][None, :]
    blended_fourier_modes = (
        spectrum * w_spec + north_row * spec_prev + south_row * spec_next
    ).astype(jnp.bfloat16)
    azimuth = jnp.dot(inverse, blended_fourier_modes, preferred_element_type=jnp.float32).astype(
        jnp.bfloat16
    )
    before_nonlinearity = jnp.dot(azimuth, w_mix, preferred_element_type=jnp.float32)
    predicted_state = (
        resampled_field.astype(jnp.float32) + jax.nn.silu(before_nonlinearity)
    ).astype(jnp.bfloat16)
    grad_pre = (loss_sensitivity[0].astype(jnp.float32) * silu_grad(before_nonlinearity)).astype(
        jnp.bfloat16
    )
    mix_local = jnp.dot(azimuth.T, grad_pre, preferred_element_type=jnp.float32)
    gridding_factor = 1.0 / math.sqrt(devices * LON)
    grad_az = jnp.dot(grad_pre, w_mix.T, preferred_element_type=jnp.float32).astype(jnp.bfloat16)
    blend_matrix_slope_local = jnp.dot(inverse.T, grad_az, preferred_element_type=jnp.float32)
    from_next = from_behind(north_row * blend_matrix_slope_local, ("enc", "blk"), -1)
    from_prev = from_behind(south_row * blend_matrix_slope_local, ("enc", "blk"), 1)
    grad_spec = (w_spec * blend_matrix_slope_local + from_next + from_prev).astype(jnp.bfloat16)
    grad_grid = loss_sensitivity[0].astype(jnp.float32) + jnp.dot(
        forward.T, grad_spec, preferred_element_type=jnp.float32
    )
    scaled = (grad_grid / denom).astype(jnp.bfloat16)
    grad_rows = jnp.dot(onehot.T, scaled, preferred_element_type=jnp.float32).astype(jnp.bfloat16)
    returned = lax.all_to_all(
        lax.all_to_all(
            grad_rows.reshape(enc_count, blk_count, CAP, CODE_BREADTH),
            "enc",
            split_axis=0,
            concat_axis=0,
            tiled=True,
        ),
        "blk",
        split_axis=1,
        concat_axis=1,
        tiled=True,
    )
    grad_latent = returned.reshape(slot_total, CODE_BREADTH)
    in_local, out_local, observation_slope = encoder_grads(
        observations, pre1, hidden, grad_latent, w_in, w_out
    )
    observed_factor = 1.0 / math.sqrt(devices * slot_total)
    input_gradient_total, output_gradient_total, blend_matrix_slope_summed = lax.psum(
        (in_local, out_local, mix_local), ("enc", "blk")
    )
    return (
        predicted_state[None],
        input_gradient_total * observed_factor,
        output_gradient_total * observed_factor,
        blend_matrix_slope_summed * gridding_factor,
        observation_slope,
    )


def solution(mesh):
    placed = (
        P(("enc", "blk"), None),
        P(("enc", "blk"), None),
        P(("enc", "blk"), None),
        P(),
        P(),
        P(),
        P(("enc", "blk"), None),
        P(("enc", "blk"), None),
        P(),
        P(("enc", "blk"), None, None),
    )
    return jax.shard_map(
        shards,
        mesh=mesh,
        in_specs=placed,
        out_specs=(P(("enc", "blk"), None, None), P(), P(), P(), P(("enc", "blk"), None)),
        check_vma=False,
    )
```

profile of v0, /device:TPU:8, one launch (start us, length us, event | category | flops | bytes accessed | tf_op | source)
XLA Modules:
  0.0 426.9 jit_solution(8997733929521939271)
XLA Ops:
  7.2 0.0 copy-start
  7.2 1.3 fusion.52
  8.5 0.0 copy-start.2
  8.5 1.0 copy-done.2
  9.5 1.5 convolution_convert_fusion.2
  11.0 0.2 reshape.48
  11.2 0.0 copy-start.11
  11.2 0.0 copy-start.19
  11.2 17.3 %all_to_all.20 = bf16[16,16,2,512]{3,2,1,0:T(2,128)(2,1)S(1)} all-to-all(bf16[16,16,2,512]{3,2,1,0:T(2,128)(2,1)S(1)} %reshape.48), channel_id=1, replica_groups=mesh['enc'=16,'blk'=16] {'enc'}, dimensions={0} | all-to-all | bytes 1048576 | tf_op jit(solution)/shard_map/all_to_all | solution.py:82
  28.5 1.3 copy.30
  29.8 8.6 %all-to-all-start.1 = ((bf16[16,16,2,512]{3,2,0,1:T(2,128)(2,1)}), bf16[16,16,2,512]{3,2,0,1:T(2,128)(2,1)S(1)}, u32[]{:S(2)}, u32[]{:S(2)}) async-start(bf16[16,16,2,512]{3,2,0,1:T(2,128)(2,1)} %copy.30), calls=%async_computation.1 | async-start | bytes 1048576 | tf_op jit(solution)/shard_map/all_to_all | solution.py:81
  38.4 0.0 copy-done.11
  38.4 0.1 iota_compare_fusion.1
  38.5 0.1 lt.38
  38.7 0.6 convert_reduce_fusion
  39.2 15.2 %all-to-all-done.1 = bf16[16,16,2,512]{3,2,0,1:T(2,128)(2,1)S(1)} async-done(((bf16[16,16,2,512]{3,2,0,1:T(2,128)(2,1)}), bf16[16,16,2,512]{3,2,0,1:T(2,128)(2,1)S(1)}, u32[]{:S(2)}, u32[]{:S(2)}) %all-to-all-start.1) | async-done | bytes 524320 | tf_op jit(solution)/shard_map/all_to_all | solution.py:81
  54.4 0.5 copy.31
  54.9 0.2 reshape.49
  55.1 1.0 divide_convert_fusion.1
  56.1 0.0 copy-start.12
  56.1 0.0 copy-start.14
  56.1 2.9 collective-permute-start.1
  59.1 2.7 collective-permute-start
  61.8 3.5 fusion.44
  65.3 4.1 multiply_convert_fusion.2
  69.4 0.0 copy-done.14
  69.4 1.4 convolution_multiply_fusion.1
  70.8 5.2 %collective-permute-done.1 = bf16[1,1440,512]{2,1,0:T(8,128)(2,1)S(1)} collective-permute-done((bf16[1,1440,512]{2,1,0:T(8,128)(2,1)S(1)}, bf16[1,1440,512]{2,1,0:T(8,128)(2,1)S(1)}, u32[]{:S(2)}, u32[]{:S(2)}) %collective-permute-start.1) | collective-permute-done | bytes 1474592 | tf_op jit(solution)/shard_map/ppermute | solution.py:21
  76.0 1.4 fusion.24
  77.3 4.6 %collective-permute-done = bf16[1,1440,512]{2,1,0:T(8,128)(2,1)S(1)} collective-permute-done((bf16[1,1440,512]{2,1,0:T(8,128)(2,1)S(1)}, bf16[1,1440,512]{2,1,0:T(8,128)(2,1)S(1)}, u32[]{:S(2)}, u32[]{:S(2)}) %collective-permute-start) | collective-permute-done | bytes 1474592 | tf_op jit(solution)/shard_map/ppermute | solution.py:18
  81.9 1.1 copy-done.13
  83.0 0.0 copy-done.18
  83.0 2.9 convolution_convert_fusion.1
  85.9 5.2 %fusion = (bf16[1440,512]{1,0:T(8,128)(2,1)S(1)}, bf16[1,1440,512]{2,1,0:T(8,128)(2,1)}) fusion(bf16[1,1440,512]{2,1,0:T(8,128)(2,1)} %param.19, bf16[1440,512]{1,0:T(8,128)(2,1)} %copy-done.12, bf16[1440,512]{1,0:T(8,128)(2,1)S(1)} %convolution_convert_fusion.1, bf16[512,512]{1,0:T(8,128)(2,1)S(1)} %copy-done), kind=kOutput, calls=%fused_computation.4 | convolution fusion | flops 765296640 | bytes 7897088 | tf_op jit(solution)/shard_map/dot_general | solution.py:105
  91.1 4.2 broadcast_multiply_fusion.3
  95.3 0.0 copy-done.1
  95.3 1.9 collective-permute-start.2
  97.2 2.6 collective-permute-start.3
  99.8 4.4 %collective-permute-done.2 = f32[256,512]{1,0:T(8,128)S(1)} collective-permute-done((f32[256,512]{1,0:T(8,128)}, f32[256,512]{1,0:T(8,128)S(1)}, u32[]{:S(2)}, u32[]{:S(2)}) %collective-permute-start.2) | collective-permute-done | bytes 524320 | tf_op jit(solution)/shard_map/ppermute | solution.py:29
  104.2 5.8 %collective-permute-done.3 = f32[256,512]{1,0:T(8,128)S(1)} collective-permute-done((f32[256,512]{1,0:T(8,128)}, f32[256,512]{1,0:T(8,128)S(1)}, u32[]{:S(2)}, u32[]{:S(2)}) %collective-permute-start.3) | collective-permute-done | bytes 524320 | tf_op jit(solution)/shard_map/ppermute | solution.py:29
  110.1 0.8 copy-done.16
  110.8 3.9 fusion.17
  114.7 0.2 reshape.50
  115.0 16.4 %all_to_all.21 = bf16[16,16,2,512]{3,2,1,0:T(2,128)(2,1)S(1)} all-to-all(bf16[16,16,2,512]{3,2,1,0:T(2,128)(2,1)S(1)} %reshape.50), channel_id=1, replica_groups=mesh['enc'=16,'blk'=16] {'enc'}, dimensions={0} | all-to-all | bytes 1048576 | tf_op jit(solution)/shard_map/all_to_all | solution.py:125
  131.3 1.3 copy.32
  132.6 3.6 all-to-all-start.3
  136.2 0.0 all-reduce.3.cloned.1.call-start
  136.2 3.3 fusion.53
  139.6 12.5 %all-to-all-done.3 = bf16[16,16,2,512]{3,2,0,1:T(2,128)(2,1)S(1)} async-done(((bf16[16,16,2,512]{3,2,0,1:T(2,128)(2,1)}), bf16[16,16,2,512]{3,2,0,1:T(2,128)(2,1)S(1)}, u32[]{:S(2)}, u32[]{:S(2)}) %all-to-all-start.3) | async-done | bytes 524320 | tf_op jit(solution)/shard_map/all_to_all | solution.py:124
  152.1 0.5 copy.33
  152.6 0.2 reshape.51
  152.8 0.0 copy-start.3
  152.8 2.0 fusion.20
  154.8 0.0 copy-done.3
  154.8 0.0 copy-start.6
  154.8 1.5 fusion.51
  156.3 1.0 convolution_bitcast_fusion
  157.3 0.0 all-reduce.3.cloned.1.call-update
  157.4 0.9 convolution_convert_fusion.3
  158.3 257.6 %all-reduce.3.cloned.1.call-done = (f32[128,512]{0,1:T(8,128)}, f32[512,512]{1,0:T(8,128)}, f32[512,512]{1,0:T(8,128)}) async-done(((f32[128,512]{0,1:T(8,128)}, f32[512,512]{1,0:T(8,128)}, f32[512,512]{1,0:T(8,128)}), (f32[128,512]{0,1:T(8,128)}, f32[512,512]{1,0:T(8,128)}, f32[512,512]{1,0:T(8,128)})) %all-reduce.3.cloned.1.call-update) | async-done | bytes 2359312 | tf_op jit(solution)/shard_map/psum | solution.py:142
  415.9 1.1 broadcast_multiply_fusion.4
  417.0 0.8 copy.34
  417.8 1.1 broadcast_multiply_fusion.1
  418.9 1.1 broadcast_multiply_fusion
  (26 shorter events, 0.1 us)
Async XLA Ops:
  7.2 78.7 %copy-start = (bf16[512,512]{1,0:T(8,128)(2,1)S(1)}, bf16[512,512]{1,0:T(8,128)(2,1)}, u32[]{:S(2)}) copy-start(bf16[512,512]{1,0:T(8,128)(2,1)} %param.18) | copy-start | bytes 1572868
  8.5 1.0 copy-start.2
  11.2 27.2 %copy-start.11 = (s32[1,256]{1,0:T(1,128)S(1)}, s32[1,256]{1,0:T(1,128)}, u32[]{:S(2)}) copy-start(s32[1,256]{1,0:T(1,128)} %param.12) | copy-start | bytes 3076
  11.2 27.5 %copy-start.19 = (s32[1,512]{1,0:T(1,128)S(1)}, s32[1,512]{1,0:T(1,128)}, u32[]{:S(2)}) copy-start(s32[1,512]{1,0:T(1,128)} %param.11) | copy-start | bytes 6148
  29.8 24.6 %all-to-all-start.1 = ((bf16[16,16,2,512]{3,2,0,1:T(2,128)(2,1)}), bf16[16,16,2,512]{3,2,0,1:T(2,128)(2,1)S(1)}, u32[]{:S(2)}, u32[]{:S(2)}) async-start(bf16[16,16,2,512]{3,2,0,1:T(2,128)(2,1)} %copy.30), calls=%async_computation.1 | async-start | bytes 1048576 | tf_op jit(solution)/shard_map/all_to_all | solution.py:81
  56.1 14.7 %copy-start.12 = (bf16[1440,512]{1,0:T(8,128)(2,1)}, bf16[1440,512]{1,0:T(8,128)(2,1)S(1)}, u32[]{:S(2)}) copy-start(bf16[1440,512]{1,0:T(8,128)(2,1)S(1)} %divide_convert_fusion.1) | copy-start | bytes 4423684
  56.1 13.3 %copy-start.14 = (f32[256,512]{1,0:T(8,128)S(1)}, f32[256,512]{1,0:T(8,128)}, u32[]{:S(2)}) copy-start(f32[256,512]{1,0:T(8,128)} %param.15) | copy-start | bytes 1572868
  56.1 19.8 %collective-permute-start.1 = (bf16[1,1440,512]{2,1,0:T(8,128)(2,1)S(1)}, bf16[1,1440,512]{2,1,0:T(8,128)(2,1)S(1)}, u32[]{:S(2)}, u32[]{:S(2)}) collective-permute-start(bf16[1,1440,512]{2,1,0:T(8,128)(2,1)S(1)} %bitcast.52), channel_id=1, source_target_pairs={{1,0},{2,1},{3,2},{4,3},{5,4},{6,5},{7,6},{8,7},{9,8},{10,9},{11,1... | collective-permute-start | bytes 4423688 | tf_op jit(solution)/shard_map/ppermute | solution.py:21
  59.1 22.8 %collective-permute-start = (bf16[1,1440,512]{2,1,0:T(8,128)(2,1)S(1)}, bf16[1,1440,512]{2,1,0:T(8,128)(2,1)S(1)}, u32[]{:S(2)}, u32[]{:S(2)}) collective-permute-start(bf16[1,1440,512]{2,1,0:T(8,128)(2,1)S(1)} %bitcast.53), channel_id=1, source_target_pairs={{0,1},{1,2},{2,3},{3,4},{4,5},{5,6},{6,7},{7,8},{8,9},{9,10},{10,1... | collective-permute-start | bytes 4423688 | tf_op jit(solution)/shard_map/ppermute | solution.py:18
  65.3 17.7 %copy-start.8 = (bf16[128,1440]{1,0:T(8,128)(2,1)}, bf16[128,1440]{1,0:T(8,128)(2,1)S(1)}, u32[]{:S(2)}) copy-start(bf16[128,1440]{1,0:T(8,128)(2,1)S(1)} %get-tuple-element.45) | copy-start | bytes 1105924
  65.3 17.7 %copy-start.9 = (bf16[128,1440]{1,0:T(8,128)(2,1)}, bf16[128,1440]{1,0:T(8,128)(2,1)S(1)}, u32[]{:S(2)}) copy-start(bf16[128,1440]{1,0:T(8,128)(2,1)S(1)} %get-tuple-element.46) | copy-start | bytes 1105924
  69.4 13.6 %copy-start.10 = (bf16[128,1440]{1,0:T(8,128)(2,1)}, bf16[128,1440]{1,0:T(8,128)(2,1)S(1)}, u32[]{:S(2)}) copy-start(bf16[128,1440]{1,0:T(8,128)(2,1)S(1)} %get-tuple-element.42) | copy-start | bytes 1105924
  69.4 6.5 %copy-start.17 = (f32[1,512]{1,0:T(1,128)S(1)}, f32[1,512]{1,0:T(1,128)}, u32[]{:S(2)}) copy-start(f32[1,512]{1,0:T(1,128)} %param.17) | copy-start | bytes 6148
  76.0 7.1 %copy-start.18 = (f32[1,512]{1,0:T(1,128)S(1)}, f32[1,512]{1,0:T(1,128)}, u32[]{:S(2)}) copy-start(f32[1,512]{1,0:T(1,128)} %param.16) | copy-start | bytes 6148
  81.9 1.1 copy-start.13
  91.1 4.2 copy-start.1
  95.3 8.9 %collective-permute-start.2 = (f32[256,512]{1,0:T(8,128)}, f32[256,512]{1,0:T(8,128)S(1)}, u32[]{:S(2)}, u32[]{:S(2)}) collective-permute-start(f32[256,512]{1,0:T(8,128)} %get-tuple-element.40), channel_id=1, source_target_pairs={{1,0},{2,1},{3,2},{4,3},{5,4},{6,5},{7,6},{8,7},{9,8},{10,9},{11,1... | collective-permute-start | bytes 1572872 | tf_op jit(solution)/shard_map/ppermute | solution.py:29
  97.2 12.8 %collective-permute-start.3 = (f32[256,512]{1,0:T(8,128)}, f32[256,512]{1,0:T(8,128)S(1)}, u32[]{:S(2)}, u32[]{:S(2)}) collective-permute-start(f32[256,512]{1,0:T(8,128)} %get-tuple-element.41), channel_id=1, source_target_pairs={{0,1},{1,2},{2,3},{3,4},{4,5},{5,6},{6,7},{7,8},{8,9},{9,10},{10,1... | collective-permute-start | bytes 1572872 | tf_op jit(solution)/shard_map/ppermute | solution.py:29
  110.1 0.8 copy-start.16
  132.6 19.5 %all-to-all-start.3 = ((bf16[16,16,2,512]{3,2,0,1:T(2,128)(2,1)}), bf16[16,16,2,512]{3,2,0,1:T(2,128)(2,1)S(1)}, u32[]{:S(2)}, u32[]{:S(2)}) async-start(bf16[16,16,2,512]{3,2,0,1:T(2,128)(2,1)} %copy.32), calls=%async_computation.3 | async-start | bytes 1048576 | tf_op jit(solution)/shard_map/all_to_all | solution.py:124
  136.2 279.7 %all-reduce.3.cloned.1.call-start = ((), (), s32[]{:S(2)}) async-start(), calls=%async_computation.4 | async-start | bytes 4718592 | tf_op jit(solution)/shard_map/psum | solution.py:142
  139.6 13.2 %copy-start.15 = (bf16[512,512]{1,0:T(8,128)(2,1)S(1)}, bf16[512,512]{1,0:T(8,128)(2,1)}, u32[]{:S(2)}) copy-start(bf16[512,512]{1,0:T(8,128)(2,1)} %param.14) | copy-start | bytes 1572868
  152.8 2.0 copy-start.3
  154.8 1.5 copy-start.6
  156.3 1.1 copy-start.7
  415.9 2.0 copy-start.5
  415.9 3.1 copy-start.4
Sparse Core Ops, SparseCore 0:
  157.5 258.3 all-reduce.2
where the time goes:
time: 428 us; the launch traced here: 427 us
  waiting for transfers between devices  305 us (71%)
  blocking collectives  33.7 us (8%)
  matrix products  31.5 us (7%)
  starting transfers between devices  22.3 us (5%)
  between operations  14.3 us (3%)
  other arithmetic  11.5 us (3%)
  local copies, waits for them, and re-layouts  8.33 us (2%)
    psum x1, waiting for transfers between devices, shards(): lax.psum((in_local, out_local, mix_local), ('enc', 'blk'))  258 us
    all_to_all x1, blocking collectives, shards(): lax.all_to_all(outgoing, 'enc', split_axis=0, concat_axis=0, tiled=True)  17.3 us
    all_to_all x1, blocking collectives, shards(): lax.all_to_all(grad_rows.reshape(enc_count, blk_count, CAP, CODE_BREADTH)...  16.4 us
    all_to_all x1, waiting for transfers between devices, shards(): lax.all_to_all(lax.all_to_all(outgoing, 'enc', split_axis=0, concat_axis=...  15.2 us
    all_to_all x1, waiting for transfers between devices, shards(): lax.all_to_all(lax.all_to_all(grad_rows.reshape(enc_count, blk_count, CAP...  12.5 us
    ppermute x2, waiting for transfers between devices, from_behind(): lax.ppermute(value, axis, [(source, source + steps) for source in range(i...  10.2 us
    all_to_all x1, starting transfers between devices, shards(): lax.all_to_all(lax.all_to_all(outgoing, 'enc', split_axis=0, concat_axis=...  8.58 us
  transfers between devices with their start and end apart: 7, of which 7 were waited for; matrix products, arithmetic and copies ran while one was open for 4% of the time, Pallas kernels for 0%

commit v1 on v0

--- a/solution.py
+++ b/solution.py
@@ -1,3 +1,4 @@
+import functools
 import math
 import jax
 import jax.numpy as jnp
@@ -8,6 +9,15 @@
 LON = 1440
 MODES = 128
 CAP = 2
+
+
+def convert_words(packet, which_axis, mesh_name):
+    for k0 in (which_axis, mesh_name):
+        packet = lax.psum(packet, k0)
+    return packet
+
+
+_wait_trees = functools.partial(convert_words, which_axis="blk", mesh_name="enc")
 
 
 def extended(block, sides, width):
@@ -139,8 +149,8 @@
         observations, pre1, hidden, grad_latent, w_in, w_out
     )
     observed_factor = 1.0 / math.sqrt(devices * slot_total)
-    input_gradient_total, output_gradient_total, blend_matrix_slope_summed = lax.psum(
-        (in_local, out_local, mix_local), ("enc", "blk")
+    input_gradient_total, output_gradient_total, blend_matrix_slope_summed = _wait_trees(
+        (in_local, out_local, mix_local)
     )
     return (
         predicted_state[None],

time: 428 us -> 388 us (0.907)
  waiting for transfers between devices: 305 us -> 264 us
    psum x1 -> x2, waiting for transfers between devices: 258 us -> 217 us  [convert_words(): packet = lax.psum(packet, k0)]
  transfers between devices with their start and end apart: 7 -> 8, of which waited for: 7 -> 8; matrix products, arithmetic and copies ran while one was open for 4% -> 4% of each run, Pallas kernels for 0% -> 0%
where the time goes in v1:
time: 388 us; the launch traced here: 386 us
  waiting for transfers between devices  264 us (68%)
  blocking collectives  33.7 us (9%)
  matrix products  31.5 us (8%)
  starting transfers between devices  22.4 us (6%)
  between operations  14.4 us (4%)
  other arithmetic  11.5 us (3%)
  local copies, waits for them, and re-layouts  8.33 us (2%)
    psum x2, waiting for transfers between devices, convert_words(): packet = lax.psum(packet, k0)  217 us
    all_to_all x1, blocking collectives, shards(): lax.all_to_all(outgoing, 'enc', split_axis=0, concat_axis=0, tiled=True)  17.3 us
    all_to_all x1, blocking collectives, shards(): lax.all_to_all(grad_rows.reshape(enc_count, blk_count, CAP, CODE_BREADTH)...  16.4 us
    all_to_all x1, waiting for transfers between devices, shards(): lax.all_to_all(lax.all_to_all(outgoing, 'enc', split_axis=0, concat_axis=...  15.2 us
    all_to_all x1, waiting for transfers between devices, shards(): lax.all_to_all(lax.all_to_all(grad_rows.reshape(enc_count, blk_count, CAP...  12.5 us
    ppermute x2, waiting for transfers between devices, from_behind(): lax.ppermute(value, axis, [(source, source + steps) for source in range(i...  10.2 us
    all_to_all x1, starting transfers between devices, shards(): lax.all_to_all(lax.all_to_all(outgoing, 'enc', split_axis=0, concat_axis=...  8.58 us
  transfers between devices with their start and end apart: 8, of which 8 were waited for; matrix products, arithmetic and copies ran while one was open for 4% of the time, Pallas kernels for 0%

profile of v1, /device:TPU:8, one launch (start us, length us, event | category | flops | bytes accessed | tf_op | source)
XLA Modules:
  0.0 386.1 jit_solution(11060997996489895265)
XLA Ops:
  7.2 0.0 copy-start
  7.2 1.3 fusion.52
  8.5 0.0 copy-start.2
  8.5 1.0 copy-done.2
  9.5 1.5 convolution_convert_fusion.2
  11.0 0.2 reshape.48
  11.2 0.0 copy-start.11
  11.2 0.0 copy-start.19
  11.2 17.3 %all_to_all.20 = bf16[16,16,2,512]{3,2,1,0:T(2,128)(2,1)S(1)} all-to-all(bf16[16,16,2,512]{3,2,1,0:T(2,128)(2,1)S(1)} %reshape.48), channel_id=1, replica_groups=mesh['enc'=16,'blk'=16] {'enc'}, dimensions={0} | all-to-all | bytes 1048576 | tf_op jit(solution)/shard_map/all_to_all | solution.py:92
  28.5 1.3 copy.30
  29.8 8.6 %all-to-all-start.1 = ((bf16[16,16,2,512]{3,2,0,1:T(2,128)(2,1)}), bf16[16,16,2,512]{3,2,0,1:T(2,128)(2,1)S(1)}, u32[]{:S(2)}, u32[]{:S(2)}) async-start(bf16[16,16,2,512]{3,2,0,1:T(2,128)(2,1)} %copy.30), calls=%async_computation.1 | async-start | bytes 1048576 | tf_op jit(solution)/shard_map/all_to_all | solution.py:91
  38.4 0.0 copy-done.11
  38.4 0.1 iota_compare_fusion.1
  38.5 0.1 lt.38
  38.7 0.6 convert_reduce_fusion
  39.2 15.2 %all-to-all-done.1 = bf16[16,16,2,512]{3,2,0,1:T(2,128)(2,1)S(1)} async-done(((bf16[16,16,2,512]{3,2,0,1:T(2,128)(2,1)}), bf16[16,16,2,512]{3,2,0,1:T(2,128)(2,1)S(1)}, u32[]{:S(2)}, u32[]{:S(2)}) %all-to-all-start.1) | async-done | bytes 524320 | tf_op jit(solution)/shard_map/all_to_all | solution.py:91
  54.4 0.5 copy.31
  54.9 0.2 reshape.49
  55.1 1.0 divide_convert_fusion.1
  56.1 0.0 copy-start.12
  56.1 0.0 copy-start.14
  56.1 2.9 collective-permute-start.1
  59.1 2.7 collective-permute-start
  61.8 3.5 fusion.44
  65.3 4.1 %multiply_convert_fusion.2 = (bf16[128,1440]{1,0:T(8,128)(2,1)S(1)}, bf16[128,1440]{1,0:T(8,128)(2,1)}) fusion(f32[128]{0:T(128)S(1)} %fusion.48), kind=kLoop, calls=%fused_computation.45 | loop fusion | flops 2580480 | bytes 737792 | tf_op jit(solution)/shard_map/convert.3
  69.4 1.4 convolution_multiply_fusion.1
  70.8 5.1 %collective-permute-done.1 = bf16[1,1440,512]{2,1,0:T(8,128)(2,1)S(1)} collective-permute-done((bf16[1,1440,512]{2,1,0:T(8,128)(2,1)S(1)}, bf16[1,1440,512]{2,1,0:T(8,128)(2,1)S(1)}, u32[]{:S(2)}, u32[]{:S(2)}) %collective-permute-start.1) | collective-permute-done | bytes 1474592 | tf_op jit(solution)/shard_map/ppermute | solution.py:31
  76.0 1.4 fusion.24
  77.3 4.6 %collective-permute-done = bf16[1,1440,512]{2,1,0:T(8,128)(2,1)S(1)} collective-permute-done((bf16[1,1440,512]{2,1,0:T(8,128)(2,1)S(1)}, bf16[1,1440,512]{2,1,0:T(8,128)(2,1)S(1)}, u32[]{:S(2)}, u32[]{:S(2)}) %collective-permute-start) | collective-permute-done | bytes 1474592 | tf_op jit(solution)/shard_map/ppermute | solution.py:28
  81.9 1.1 copy-done.13
  83.1 2.9 convolution_convert_fusion.1
  85.9 5.2 %fusion = (bf16[1440,512]{1,0:T(8,128)(2,1)S(1)}, bf16[1,1440,512]{2,1,0:T(8,128)(2,1)}) fusion(bf16[1,1440,512]{2,1,0:T(8,128)(2,1)} %param.19, bf16[1440,512]{1,0:T(8,128)(2,1)} %copy-done.12, bf16[1440,512]{1,0:T(8,128)(2,1)S(1)} %convolution_convert_fusion.1, bf16[512,512]{1,0:T(8,128)(2,1)S(1)} %copy-done), kind=kOutput, calls=%fused_computation.4 | convolution fusion | flops 765296640 | bytes 7897088 | tf_op jit(solution)/shard_map/dot_general | solution.py:115
  91.1 4.2 %broadcast_multiply_fusion.3 = (f32[256,512]{1,0:T(8,128)}, f32[256,512]{1,0:T(8,128)}, f32[256,512]{1,0:T(8,128)}) fusion(f32[512]{0:T(512)S(1)} %bitcast.57, f32[512]{0:T(512)S(1)} %bitcast.55, bf16[1440,512]{1,0:T(8,128)(2,1)S(1)} %get-tuple-element.41, bf16[512,512]{1,0:T(8,128)(2,1)S(1)} %copy-done, bf16[128,1440]{1,0:T(8,128)(2,1)} %get-tuple-element.46, ...), kind=kOutput, calls=%fused_computation.57 | convolution fusion | flops 1134936064 | bytes 4313088 | tf_op jit(solution)/shard_map/dot_general | solution.py:125
  95.3 1.9 collective-permute-start.2
  97.2 2.6 collective-permute-start.3
  99.8 4.4 %collective-permute-done.2 = f32[256,512]{1,0:T(8,128)S(1)} collective-permute-done((f32[256,512]{1,0:T(8,128)}, f32[256,512]{1,0:T(8,128)S(1)}, u32[]{:S(2)}, u32[]{:S(2)}) %collective-permute-start.2) | collective-permute-done | bytes 524320 | tf_op jit(solution)/shard_map/ppermute | solution.py:39
  104.2 5.8 %collective-permute-done.3 = f32[256,512]{1,0:T(8,128)S(1)} collective-permute-done((f32[256,512]{1,0:T(8,128)}, f32[256,512]{1,0:T(8,128)S(1)}, u32[]{:S(2)}, u32[]{:S(2)}) %collective-permute-start.3) | collective-permute-done | bytes 524320 | tf_op jit(solution)/shard_map/ppermute | solution.py:39
  110.1 0.8 copy-done.16
  110.9 3.9 %fusion.17 = bf16[512,512]{1,0:T(8,128)(2,1)S(1)} fusion(s32[512]{0:T(512)S(1)} %bitcast.60, pred[512]{0:T(512)(128)(4,1)S(1)} %lt.38, bf16[1,1440,512]{2,1,0:T(8,128)(2,1)} %param.19, f32[1440]{0:T(1024)S(1)} %broadcast_maximum_fusion, f32[256,512]{1,0:T(8,128)} %copy-done.16, f32[256,512]{1,0:T(8,128)S(1)} %collective-permute-done.2, ...), kind=kOutput, calls=%fused_computation.24 | convolution fusion | flops 1139146752 | bytes 4841600 | tf_op jit(solution)/shard_map/dot_general | solution.py:133
  114.8 0.2 reshape.50
  115.0 16.4 %all_to_all.21 = bf16[16,16,2,512]{3,2,1,0:T(2,128)(2,1)S(1)} all-to-all(bf16[16,16,2,512]{3,2,1,0:T(2,128)(2,1)S(1)} %reshape.50), channel_id=1, replica_groups=mesh['enc'=16,'blk'=16] {'enc'}, dimensions={0} | all-to-all | bytes 1048576 | tf_op jit(solution)/shard_map/all_to_all | solution.py:135
  131.3 1.3 copy.32
  132.6 3.6 all-to-all-start.3
  136.2 0.0 all-reduce.5.cloned.1.call-start
  136.2 3.4 fusion.53
  139.6 12.5 %all-to-all-done.3 = bf16[16,16,2,512]{3,2,0,1:T(2,128)(2,1)S(1)} async-done(((bf16[16,16,2,512]{3,2,0,1:T(2,128)(2,1)}), bf16[16,16,2,512]{3,2,0,1:T(2,128)(2,1)S(1)}, u32[]{:S(2)}, u32[]{:S(2)}) %all-to-all-start.3) | async-done | bytes 524320 | tf_op jit(solution)/shard_map/all_to_all | solution.py:134
  152.1 0.5 copy.33
  152.6 0.2 reshape.51
  152.8 0.0 copy-start.3
  152.8 2.0 fusion.20
  154.8 0.0 copy-start.6
  154.8 1.5 fusion.51
  156.3 1.0 convolution_bitcast_fusion
  157.3 0.0 all-reduce.5.cloned.1.call-update
  157.4 0.0 copy-start.7
  157.4 0.0 all-reduce.7.cloned.1.call-start
  157.4 112.3 %all-reduce.5.cloned.1.call-done = (f32[128,512]{0,1:T(8,128)}, f32[512,512]{1,0:T(8,128)}, f32[512,512]{1,0:T(8,128)}) async-done(((f32[128,512]{0,1:T(8,128)}, f32[512,512]{1,0:T(8,128)}, f32[512,512]{1,0:T(8,128)}), (f32[128,512]{0,1:T(8,128)}, f32[512,512]{1,0:T(8,128)}, f32[512,512]{1,0:T(8,128)})) %all-reduce.5.cloned.1.call-update) | async-done | bytes 2359312 | tf_op jit(solution)/shard_map/psum | solution.py:16
  269.7 0.0 all-reduce.7.cloned.1.call-update
  269.7 1.0 convolution_convert_fusion.3
  270.7 104.4 %all-reduce.7.cloned.1.call-done = (f32[128,512]{0,1:T(8,128)}, f32[512,512]{1,0:T(8,128)}, f32[512,512]{1,0:T(8,128)}) async-done(((f32[128,512]{0,1:T(8,128)}, f32[512,512]{1,0:T(8,128)}, f32[512,512]{1,0:T(8,128)}), (f32[128,512]{0,1:T(8,128)}, f32[512,512]{1,0:T(8,128)}, f32[512,512]{1,0:T(8,128)})) %all-reduce.7.cloned.1.call-update) | async-done | bytes 2359312 | tf_op jit(solution)/shard_map/psum | solution.py:16
  375.1 1.1 broadcast_multiply_fusion.4
  376.2 0.8 copy.34
  377.1 1.1 broadcast_multiply_fusion.1
  378.2 1.1 broadcast_multiply_fusion
  (29 shorter events, 0.1 us)
Async XLA Ops:
  7.2 78.7 %copy-start = (bf16[512,512]{1,0:T(8,128)(2,1)S(1)}, bf16[512,512]{1,0:T(8,128)(2,1)}, u32[]{:S(2)}) copy-start(bf16[512,512]{1,0:T(8,128)(2,1)} %param.18) | copy-start | bytes 1572868
  8.5 1.0 copy-start.2
  11.2 27.2 %copy-start.11 = (s32[1,256]{1,0:T(1,128)S(1)}, s32[1,256]{1,0:T(1,128)}, u32[]{:S(2)}) copy-start(s32[1,256]{1,0:T(1,128)} %param.12) | copy-start | bytes 3076
  11.2 27.5 %copy-start.19 = (s32[1,512]{1,0:T(1,128)S(1)}, s32[1,512]{1,0:T(1,128)}, u32[]{:S(2)}) copy-start(s32[1,512]{1,0:T(1,128)} %param.11) | copy-start | bytes 6148
  29.8 24.6 %all-to-all-start.1 = ((bf16[16,16,2,512]{3,2,0,1:T(2,128)(2,1)}), bf16[16,16,2,512]{3,2,0,1:T(2,128)(2,1)S(1)}, u32[]{:S(2)}, u32[]{:S(2)}) async-start(bf16[16,16,2,512]{3,2,0,1:T(2,128)(2,1)} %copy.30), calls=%async_computation.1 | async-start | bytes 1048576 | tf_op jit(solution)/shard_map/all_to_all | solution.py:91
  56.1 14.7 %copy-start.12 = (bf16[1440,512]{1,0:T(8,128)(2,1)}, bf16[1440,512]{1,0:T(8,128)(2,1)S(1)}, u32[]{:S(2)}) copy-start(bf16[1440,512]{1,0:T(8,128)(2,1)S(1)} %divide_convert_fusion.1) | copy-start | bytes 4423684
  56.1 13.3 %copy-start.14 = (f32[256,512]{1,0:T(8,128)S(1)}, f32[256,512]{1,0:T(8,128)}, u32[]{:S(2)}) copy-start(f32[256,512]{1,0:T(8,128)} %param.15) | copy-start | bytes 1572868
  56.1 19.8 %collective-permute-start.1 = (bf16[1,1440,512]{2,1,0:T(8,128)(2,1)S(1)}, bf16[1,1440,512]{2,1,0:T(8,128)(2,1)S(1)}, u32[]{:S(2)}, u32[]{:S(2)}) collective-permute-start(bf16[1,1440,512]{2,1,0:T(8,128)(2,1)S(1)} %bitcast.52), channel_id=1, source_target_pairs={{1,0},{2,1},{3,2},{4,3},{5,4},{6,5},{7,6},{8,7},{9,8},{10,9},{11,1... | collective-permute-start | bytes 4423688 | tf_op jit(solution)/shard_map/ppermute | solution.py:31
  59.1 22.8 %collective-permute-start = (bf16[1,1440,512]{2,1,0:T(8,128)(2,1)S(1)}, bf16[1,1440,512]{2,1,0:T(8,128)(2,1)S(1)}, u32[]{:S(2)}, u32[]{:S(2)}) collective-permute-start(bf16[1,1440,512]{2,1,0:T(8,128)(2,1)S(1)} %bitcast.53), channel_id=1, source_target_pairs={{0,1},{1,2},{2,3},{3,4},{4,5},{5,6},{6,7},{7,8},{8,9},{9,10},{10,1... | collective-permute-start | bytes 4423688 | tf_op jit(solution)/shard_map/ppermute | solution.py:28
  65.3 17.7 %copy-start.8 = (bf16[128,1440]{1,0:T(8,128)(2,1)}, bf16[128,1440]{1,0:T(8,128)(2,1)S(1)}, u32[]{:S(2)}) copy-start(bf16[128,1440]{1,0:T(8,128)(2,1)S(1)} %get-tuple-element.48) | copy-start | bytes 1105924
  65.3 17.7 %copy-start.9 = (bf16[128,1440]{1,0:T(8,128)(2,1)}, bf16[128,1440]{1,0:T(8,128)(2,1)S(1)}, u32[]{:S(2)}) copy-start(bf16[128,1440]{1,0:T(8,128)(2,1)S(1)} %get-tuple-element.49) | copy-start | bytes 1105924
  69.4 13.6 %copy-start.10 = (bf16[128,1440]{1,0:T(8,128)(2,1)}, bf16[128,1440]{1,0:T(8,128)(2,1)S(1)}, u32[]{:S(2)}) copy-start(bf16[128,1440]{1,0:T(8,128)(2,1)S(1)} %get-tuple-element.45) | copy-start | bytes 1105924
  69.4 6.5 %copy-start.17 = (f32[1,512]{1,0:T(1,128)S(1)}, f32[1,512]{1,0:T(1,128)}, u32[]{:S(2)}) copy-start(f32[1,512]{1,0:T(1,128)} %param.17) | copy-start | bytes 6148
  76.0 7.1 %copy-start.18 = (f32[1,512]{1,0:T(1,128)S(1)}, f32[1,512]{1,0:T(1,128)}, u32[]{:S(2)}) copy-start(f32[1,512]{1,0:T(1,128)} %param.16) | copy-start | bytes 6148
  81.9 1.1 copy-start.13
  91.1 4.2 %copy-start.1 = (bf16[1440,512]{1,0:T(8,128)(2,1)}, bf16[1440,512]{1,0:T(8,128)(2,1)S(1)}, u32[]{:S(2)}) copy-start(bf16[1440,512]{1,0:T(8,128)(2,1)S(1)} %get-tuple-element.41) | copy-start | bytes 4423684
  95.3 8.9 %collective-permute-start.2 = (f32[256,512]{1,0:T(8,128)}, f32[256,512]{1,0:T(8,128)S(1)}, u32[]{:S(2)}, u32[]{:S(2)}) collective-permute-start(f32[256,512]{1,0:T(8,128)} %get-tuple-element.43), channel_id=1, source_target_pairs={{1,0},{2,1},{3,2},{4,3},{5,4},{6,5},{7,6},{8,7},{9,8},{10,9},{11,1... | collective-permute-start | bytes 1572872 | tf_op jit(solution)/shard_map/ppermute | solution.py:39
  97.2 12.8 %collective-permute-start.3 = (f32[256,512]{1,0:T(8,128)}, f32[256,512]{1,0:T(8,128)S(1)}, u32[]{:S(2)}, u32[]{:S(2)}) collective-permute-start(f32[256,512]{1,0:T(8,128)} %get-tuple-element.44), channel_id=1, source_target_pairs={{0,1},{1,2},{2,3},{3,4},{4,5},{5,6},{6,7},{7,8},{8,9},{9,10},{10,1... | collective-permute-start | bytes 1572872 | tf_op jit(solution)/shard_map/ppermute | solution.py:39
  110.1 0.8 copy-start.16
  132.6 19.5 %all-to-all-start.3 = ((bf16[16,16,2,512]{3,2,0,1:T(2,128)(2,1)}), bf16[16,16,2,512]{3,2,0,1:T(2,128)(2,1)S(1)}, u32[]{:S(2)}, u32[]{:S(2)}) async-start(bf16[16,16,2,512]{3,2,0,1:T(2,128)(2,1)} %copy.32), calls=%async_computation.3 | async-start | bytes 1048576 | tf_op jit(solution)/shard_map/all_to_all | solution.py:134
  136.2 133.5 %all-reduce.5.cloned.1.call-start = ((), (), s32[]{:S(2)}) async-start(), calls=%async_computation.4 | async-start | bytes 4718592 | tf_op jit(solution)/shard_map/psum | solution.py:16
  139.6 13.2 %copy-start.15 = (bf16[512,512]{1,0:T(8,128)(2,1)S(1)}, bf16[512,512]{1,0:T(8,128)(2,1)}, u32[]{:S(2)}) copy-start(bf16[512,512]{1,0:T(8,128)(2,1)} %param.14) | copy-start | bytes 1572868
  152.8 2.0 copy-start.3
  154.8 1.5 copy-start.6
  157.4 112.4 %copy-start.7 = (bf16[128,512]{1,0:T(8,128)(2,1)S(1)}, bf16[128,512]{1,0:T(8,128)(2,1)}, u32[]{:S(2)}) copy-start(bf16[128,512]{1,0:T(8,128)(2,1)} %param.13) | copy-start | bytes 393220
  157.4 217.7 %all-reduce.7.cloned.1.call-start = ((), (), s32[]{:S(2)}) async-start(), calls=%async_computation.5 | async-start | bytes 4718592 | tf_op jit(solution)/shard_map/psum | solution.py:16
  375.1 2.0 copy-start.5
  375.1 3.1 copy-start.4
Sparse Core Ops, SparseCore 0:
  157.5 112.1 all-reduce.4
  273.3 101.7 all-reduce.6
